TPU v7x, 256 devices: a whole 4x4x8 slice. The times are simulated.
256 devices in a mesh: gx: 8 (over x_lo, y), gy: 4 (over x_hi, core), gz: 8 (over z).
Axes of the slice: x: 4 (x_hi: 2, x_lo: 2; x = x_hi * 2 + x_lo), y: 4, z: 8, core: 2. Of those that a mesh axis runs over, the one named last changes fastest.
Arguments:
- tokens: bfloat16 [4096, 6144], P(('gx', 'gy'), 'gz'), may hold values from -6 to 6
- weight: bfloat16 [6144, 24576], P('gz', ('gy', 'gx')), may hold values from -0.15625 to 0.15625
- cotangent: bfloat16 [4096, 24576], P('gx', ('gy', 'gz')), may hold values from -0.5 to 0.5
Outputs:
- activated: bfloat16 [4096, 24576], P('gx', ('gy', 'gz'))
- input_grad: bfloat16 [4096, 6144], P(('gx', 'gy'), 'gz')
- weight_grad: bfloat16 [6144, 24576], P('gz', ('gy', 'gx'))
All inputs are finite; a program needn't handle non-finite values.
Results may differ from a plain program's by a relative error of at most 0.023.
Values may be sent and summed in bfloat16 or wider, within the bound.
A program may use at most 128 MiB of HBM per device.

v0:
```python
import jax
import jax.numpy as jnp
from jax import lax
from jax.sharding import PartitionSpec as P

inv_root_two = 0.7071067811865476
inv_root_tau = 0.3989422804014327


def gelu_value(preact):
    return 0.5 * preact * (1.0 + jax.scipy.special.erf(preact * inv_root_two))


def gelu_slope(preact):
    return (
        0.5 * (1.0 + jax.scipy.special.erf(preact * inv_root_two))
        + preact * jnp.exp(-0.5 * preact * preact) * inv_root_tau
    )


def on_device(tokens, weight, cotangent):
    token_rows = lax.all_gather(tokens, "gy", axis=0, tiled=True)
    whole_weight = lax.all_gather(weight, "gx", axis=1, tiled=True)
    partial_value = jnp.dot(token_rows, whole_weight, preferred_element_type=jnp.float32)
    preact = lax.psum_scatter(
        partial_value.astype(jnp.bfloat16), "gz", scatter_dimension=1, tiled=True
    ).astype(jnp.float32)
    activated = gelu_value(preact).astype(jnp.bfloat16)
    grad_pre = (cotangent.astype(jnp.float32) * gelu_slope(preact)).astype(jnp.bfloat16)
    grad_block = lax.all_gather(grad_pre, "gz", axis=1, tiled=True)
    input_grad = lax.psum_scatter(
        lax.dot_general(
            grad_block, whole_weight, (((1,), (1,)), ((), ())), preferred_element_type=jnp.float32
        ).astype(jnp.bfloat16),
        "gy",
        scatter_dimension=0,
        tiled=True,
    )
    weight_part = lax.dot_general(
        token_rows, grad_block, (((0,), (0,)), ((), ())), preferred_element_type=jnp.float32
    )
    weight_grad = lax.psum_scatter(
        weight_part.astype(jnp.bfloat16), "gx", scatter_dimension=1, tiled=True
    )
    return (activated, input_grad, weight_grad)


def solution(mesh):
    in_specs = (P(("gx", "gy"), "gz"), P("gz", ("gy", "gx")), P("gx", ("gy", "gz")))
    out_specs = (P("gx", ("gy", "gz")), P(("gx", "gy"), "gz"), P("gz", ("gy", "gx")))
    return jax.shard_map(
        on_device, mesh=mesh, in_specs=in_specs, out_specs=out_specs, check_vma=False
    )
```

profile of v0, /device:TPU:1, one launch (start us, length us, event | category | flops | bytes accessed | tf_op | source)
XLA Modules:
  0.0 437.0 jit_solution(9703800722184600346)
XLA Ops:
  7.2 0.0 all-gather.3.cloned.1.call-start
  7.2 0.7 all-gather.3.cloned.1.call-update
  7.9 0.0 reduce-scatter.4.cloned.1.call-start
  7.9 12.0 %all_gather.9 = bf16[512,768]{1,0:T(8,128)(2,1)S(1)} all-gather(bf16[128,768]{1,0:T(8,128)(2,1)} %param.3), channel_id=1, replica_groups=mesh['gx'=8,'gy'=4,'gz'=8] {'gy'}, dimensions={0}, use_global_device_ids=true | all-gather | bytes 983040 | tf_op jit(solution)/shard_map/all_gather | solution.py:22
  20.0 97.9 %all-gather.3.cloned.1.call-done = bf16[768,6144]{1,0:T(8,128)(2,1)} async-done(((bf16[768,768]{1,0:T(8,128)(2,1)}), bf16[768,6144]{1,0:T(8,128)(2,1)}) %all-gather.3.cloned.1.call-update) | async-done | bytes 9437200 | tf_op jit(solution)/shard_map/all_gather | solution.py:23
  117.9 10.6 %convolution_convert_fusion.1 = bf16[512,6144]{1,0:T(8,128)(2,1)} fusion(bf16[512,768]{1,0:T(8,128)(2,1)S(1)} %all_gather.9, bf16[768,6144]{1,0:T(8,128)(2,1)} %all-gather.3.cloned.1.call-done), kind=kOutput, calls=%fused_computation.2 | convolution fusion | flops 4834983936 | bytes 16515072 | tf_op jit(solution)/shard_map/dot_general | solution.py:24
  128.4 0.0 copy-start
  128.5 0.0 reduce-scatter.4.cloned.1.call-update
  128.5 0.0 all-gather.5.cloned.1.call-start
  128.5 74.1 %reduce-scatter.4.cloned.1.call-done = bf16[512,768]{1,0:T(8,128)(2,1)} async-done(((bf16[512,6144]{1,0:T(8,128)(2,1)}), bf16[512,768]{1,0:T(8,128)(2,1)}) %reduce-scatter.4.cloned.1.call-update) | async-done | bytes 786448 | tf_op jit(solution)/shard_map/reduce_scatter | solution.py:25
  202.6 0.0 copy-done
  202.6 3.1 fusion.9
  205.8 0.0 all-gather.5.cloned.1.call-update
  205.8 0.0 reduce-scatter.8.cloned.1.call-start
  205.8 73.1 %all-gather.5.cloned.1.call-done = bf16[512,6144]{1,0:T(8,128)(2,1)} async-done(((bf16[512,768]{1,0:T(8,128)(2,1)}), bf16[512,6144]{1,0:T(8,128)(2,1)}) %all-gather.5.cloned.1.call-update) | async-done | bytes 6291472 | tf_op jit(solution)/shard_map/all_gather | solution.py:30
  279.0 10.2 %fusion = bf16[768,6144]{0,1:T(8,128)(2,1)} fusion(bf16[512,6144]{1,0:T(8,128)(2,1)} %all-gather.5.cloned.1.call-done, bf16[512,768]{1,0:T(8,128)(2,1)S(1)} %all_gather.9), kind=kOutput, calls=%fused_computation.1 | convolution fusion | flops 4836556800 | bytes 16515072 | tf_op jit(solution)/shard_map/dot_general | solution.py:39
  289.2 0.0 reduce-scatter.8.cloned.1.call-update
  289.2 0.0 reduce-scatter.6.cloned.1.call-start
  289.3 10.7 %convolution_convert_fusion.2 = bf16[512,768]{1,0:T(8,128)(2,1)} fusion(bf16[512,6144]{1,0:T(8,128)(2,1)} %all-gather.5.cloned.1.call-done, bf16[768,6144]{1,0:T(8,128)(2,1)} %all-gather.3.cloned.1.call-done), kind=kOutput, calls=%fused_computation.17 | convolution fusion | flops 4832231424 | bytes 16515072 | tf_op jit(solution)/shard_map/dot_general | solution.py:32
  300.0 0.0 reduce-scatter.6.cloned.1.call-update
  300.0 93.2 %reduce-scatter.8.cloned.1.call-done = bf16[768,768]{0,1:T(8,128)(2,1)} async-done(((bf16[768,6144]{0,1:T(8,128)(2,1)}), bf16[768,768]{0,1:T(8,128)(2,1)}) %reduce-scatter.8.cloned.1.call-update) | async-done | bytes 1179664 | tf_op jit(solution)/shard_map/reduce_scatter | solution.py:42
  393.2 2.4 copy.6
  395.6 34.9 %reduce-scatter.6.cloned.1.call-done = bf16[128,768]{1,0:T(8,128)(2,1)} async-done(((bf16[512,768]{1,0:T(8,128)(2,1)}), bf16[128,768]{1,0:T(8,128)(2,1)}) %reduce-scatter.6.cloned.1.call-update) | async-done | bytes 196624 | tf_op jit(solution)/shard_map/reduce_scatter | solution.py:31
Async XLA Ops:
  7.2 110.7 %all-gather.3.cloned.1.call-start = ((), (), s32[]{:S(2)}) async-start(), calls=%async_computation.3 | async-start | bytes 10616832 | tf_op jit(solution)/shard_map/all_gather | solution.py:23
  7.9 194.7 %reduce-scatter.4.cloned.1.call-start = ((), (), s32[]{:S(2)}) async-start(), calls=%async_computation.4 | async-start | bytes 7077888 | tf_op jit(solution)/shard_map/reduce_scatter | solution.py:25
  128.4 74.2 %copy-start = (bf16[512,768]{1,0:T(8,128)(2,1)S(1)}, bf16[512,768]{1,0:T(8,128)(2,1)}, u32[]{:S(2)}) copy-start(bf16[512,768]{1,0:T(8,128)(2,1)} %param.5) | copy-start | bytes 2359300
  128.5 150.5 %all-gather.5.cloned.1.call-start = ((), (), s32[]{:S(2)}) async-start(), calls=%async_computation.5 | async-start | bytes 7077888 | tf_op jit(solution)/shard_map/all_gather | solution.py:30
  205.8 187.4 %reduce-scatter.8.cloned.1.call-start = ((), (), s32[]{:S(2)}) async-start(), calls=%async_computation.7 | async-start | bytes 10616832 | tf_op jit(solution)/shard_map/reduce_scatter | solution.py:42
  289.2 141.3 %reduce-scatter.6.cloned.1.call-start = ((), (), s32[]{:S(2)}) async-start(), calls=%async_computation.6 | async-start | bytes 983040 | tf_op jit(solution)/shard_map/reduce_scatter | solution.py:31
Sparse Core Ops, SparseCore 0:
  9.8 108.0 all-gather.2
  128.6 73.9 reduce-scatter.3
  205.9 72.9 all-gather.4
  289.3 103.8 reduce-scatter.7
  396.4 34.0 reduce-scatter.5
where the time goes:
time: 437 us
  waiting for transfers between devices  374 us (86%)
  matrix products  31.5 us (7%)
  between operations  13.8 us (3%)
  blocking collectives  12 us (3%)
    all_gather x1, waiting for transfers between devices, on_device(): whole_weight = lax.all_gather(weight, 'gx', axis=1, tiled=True)  97.9 us
    reduce_scatter x1, waiting for transfers between devices, on_device(): lax.psum_scatter(weight_part.astype(jnp.bfloat16), 'gx', scatter_dimensio...  93.2 us
    reduce_scatter x1, waiting for transfers between devices, on_device(): lax.psum_scatter(partial_value.astype(jnp.bfloat16), 'gz', scatter_dimens...  74.1 us
    all_gather x1, waiting for transfers between devices, on_device(): grad_block = lax.all_gather(grad_pre, 'gz', axis=1, tiled=True)  73.1 us
    reduce_scatter x1, waiting for transfers between devices, on_device(): lax.psum_scatter(lax.dot_general(grad_block, whole_weight, (((1,), (1,)),...  34.9 us
    all_gather x1, blocking collectives, on_device(): token_rows = lax.all_gather(tokens, 'gy', axis=0, tiled=True)  12 us
    dot_general x1, matrix products, on_device(): lax.dot_general(grad_block, whole_weight, (((1,), (1,)), ((), ())), prefe...  10.7 us
    dot_general x1, matrix products, on_device(): jnp.dot(token_rows, whole_weight, preferred_element_type=jnp.float32)  10.6 us
  transfers between devices with their start and end apart: 5, of which 5 were waited for; matrix products, arithmetic and copies ran while one was open for 3% of the time, Pallas kernels for 0%

commit v1 on v0

v1 whole, which is shorter than its diff:
```python
import jax
import jax.numpy as jnp
from jax import lax
from jax.sharding import PartitionSpec as P

inv_root_two = 0.7071067811865476
inv_root_tau = 0.3989422804014327


def gelu_value(preact):
    return 0.5 * preact * (1.0 + jax.scipy.special.erf(preact * inv_root_two))


def gelu_slope(preact):
    return (
        0.5 * (1.0 + jax.scipy.special.erf(preact * inv_root_two))
        + preact * jnp.exp(-0.5 * preact * preact) * inv_root_tau
    )


def on_device(tokens, weight, cotangent):
    n = lax.axis_size("gz")
    swap = [(a * n + b, b * n + a) for a in range(n) for b in range(n)]
    token_rows = lax.all_gather(tokens, ("gx", "gy"), axis=0, tiled=True)
    cot = lax.ppermute(cotangent, ("gx", "gz"), swap)
    partial_value = jnp.dot(token_rows, weight, preferred_element_type=jnp.float32)
    preact = lax.psum_scatter(
        partial_value.astype(jnp.bfloat16), "gz", scatter_dimension=0, tiled=True
    ).astype(jnp.float32)
    activated = gelu_value(preact).astype(jnp.bfloat16)
    grad_pre = (cot.astype(jnp.float32) * gelu_slope(preact)).astype(jnp.bfloat16)
    activated = lax.ppermute(activated, ("gx", "gz"), swap)
    grads = lax.all_gather(grad_pre, "gz", axis=0, tiled=True)
    input_grad = lax.psum_scatter(
        lax.dot_general(
            grads, weight, (((1,), (1,)), ((), ())), preferred_element_type=jnp.float32
        ).astype(jnp.bfloat16),
        ("gx", "gy"),
        scatter_dimension=0,
        tiled=True,
    )
    weight_grad = lax.dot_general(
        token_rows, grads, (((0,), (0,)), ((), ())), preferred_element_type=jnp.float32
    ).astype(jnp.bfloat16)
    return (activated, input_grad, weight_grad)


def solution(mesh):
    in_specs = (P(("gx", "gy"), "gz"), P("gz", ("gy", "gx")), P("gx", ("gy", "gz")))
    out_specs = (P("gx", ("gy", "gz")), P(("gx", "gy"), "gz"), P("gz", ("gy", "gx")))
    return jax.shard_map(
        on_device, mesh=mesh, in_specs=in_specs, out_specs=out_specs, check_vma=False
    )
```

time: 437 us -> 541 us (1.24)
  waiting for transfers between devices: 374 us -> 488 us
  blocking collectives: 12 us -> 0 us
    reduce_scatter x2 -> x1, waiting for transfers between devices: 128 us -> 194 us  [on_device(): lax.psum_scatter(lax.dot_general(grads, weight, (((1,), (1,)), ((), ())),...]
    reduce_scatter x1, waiting for transfers between devices: 74.1 us -> 134 us  [on_device(): lax.psum_scatter(partial_value.astype(jnp.bfloat16), 'gz', scatter_dimens...]
    all_gather x2, waiting for transfers between devices: 171 us -> 158 us  [the longest x1 86.3 us: on_device(): grads = lax.all_gather(grad_pre, 'gz', axis=0, tiled=True)]
    all_gather x1 -> x0, blocking collectives: 12 us -> none  [on_device(): token_rows = lax.all_gather(tokens, 'gy', axis=0, tiled=True)]
  transfers between devices with their start and end apart: 5 -> 6, of which waited for: 5 -> 4; matrix products, arithmetic and copies ran while one was open for 3% -> 2% of each run, Pallas kernels for 0% -> 0%
where the time goes in v1:
time: 541 us; the launch traced here: 538 us
  waiting for transfers between devices  488 us (90%)
  matrix products  28.5 us (5%)
  between operations  13.8 us (3%)
    reduce_scatter x1, waiting for transfers between devices, on_device(): lax.psum_scatter(lax.dot_general(grads, weight, (((1,), (1,)), ((), ())),...  194 us
    reduce_scatter x1, waiting for transfers between devices, on_device(): lax.psum_scatter(partial_value.astype(jnp.bfloat16), 'gz', scatter_dimens...  134 us
    all_gather x1, waiting for transfers between devices, on_device(): grads = lax.all_gather(grad_pre, 'gz', axis=0, tiled=True)  86.3 us
    all_gather x1, waiting for transfers between devices, on_device(): token_rows = lax.all_gather(tokens, ('gx', 'gy'), axis=0, tiled=True)  72.1 us
  transfers between devices with their start and end apart: 6, of which 4 were waited for; matrix products, arithmetic and copies ran while one was open for 2% of the time, Pallas kernels for 0%

profile of v1, /device:TPU:1, one launch (start us, length us, event | category | flops | bytes accessed | tf_op | source)
XLA Modules:
  0.0 538.0 jit_solution(12065971609608666449)
XLA Ops:
  7.2 0.0 copy-start
  7.2 0.0 all-gather.3.cloned.1.call-start
  7.2 0.7 all-gather.3.cloned.1.call-update
  7.9 0.0 reduce-scatter.3.cloned.1.call-start
  8.0 72.1 %all-gather.3.cloned.1.call-done = bf16[4096,768]{1,0:T(8,128)(2,1)} async-done(((bf16[128,768]{1,0:T(8,128)(2,1)}), bf16[4096,768]{1,0:T(8,128)(2,1)}) %all-gather.3.cloned.1.call-update) | async-done | bytes 6291472 | tf_op jit(solution)/shard_map/all_gather | solution.py:24
  80.0 0.0 copy-done
  80.0 9.7 %convolution_convert_fusion.1 = bf16[4096,768]{1,0:T(8,128)(2,1)} fusion(bf16[4096,768]{1,0:T(8,128)(2,1)} %all-gather.3.cloned.1.call-done, bf16[768,768]{1,0:T(8,128)(2,1)S(1)} %copy-done), kind=kOutput, calls=%fused_computation.1 | convolution fusion | flops 4834983936 | bytes 13762560 | tf_op jit(solution)/shard_map/dot_general | solution.py:26
  89.7 0.0 copy-start.1
  89.8 0.0 reduce-scatter.3.cloned.1.call-update
  89.8 0.0 all-gather.5.cloned.1.call-start
  89.8 1.1 copy-done.1
  90.9 0.7 collective-permute-start.1
  91.6 0.0 collective-permute-done.1
  91.6 134.2 %reduce-scatter.3.cloned.1.call-done = bf16[512,768]{1,0:T(8,128)(2,1)} async-done(((bf16[4096,768]{1,0:T(8,128)(2,1)}), bf16[512,768]{1,0:T(8,128)(2,1)}) %reduce-scatter.3.cloned.1.call-update) | async-done | bytes 786448 | tf_op jit(solution)/shard_map/reduce_scatter | solution.py:27
  225.8 2.9 fusion.8
  228.7 0.0 all-gather.5.cloned.1.call-update
  228.7 0.0 reduce-scatter.5.cloned.1.call-start
  228.8 86.3 %all-gather.5.cloned.1.call-done = bf16[4096,768]{1,0:T(8,128)(2,1)} async-done(((bf16[512,768]{1,0:T(8,128)(2,1)}), bf16[4096,768]{1,0:T(8,128)(2,1)}) %all-gather.5.cloned.1.call-update) | async-done | bytes 6291472 | tf_op jit(solution)/shard_map/all_gather | solution.py:33
  315.1 9.7 %convolution_convert_fusion = bf16[4096,768]{1,0:T(8,128)(2,1)} fusion(bf16[4096,768]{1,0:T(8,128)(2,1)} %all-gather.5.cloned.1.call-done, bf16[768,768]{1,0:T(8,128)(2,1)S(1)} %copy-done), kind=kOutput, calls=%fused_computation | convolution fusion | flops 4834983936 | bytes 13762560 | tf_op jit(solution)/shard_map/dot_general | solution.py:35
  324.8 0.0 reduce-scatter.5.cloned.1.call-update
  324.9 0.7 collective-permute-start
  325.6 0.0 collective-permute-done
  325.6 9.1 %fusion.9 = bf16[768,768]{0,1:T(8,128)(2,1)S(1)} fusion(bf16[4096,768]{1,0:T(8,128)(2,1)} %all-gather.5.cloned.1.call-done, bf16[4096,768]{1,0:T(8,128)(2,1)} %all-gather.3.cloned.1.call-done), kind=kOutput, calls=%fused_computation.17 | convolution fusion | flops 4832428032 | bytes 13762560 | tf_op jit(solution)/shard_map/dot_general | solution.py:42
  334.7 1.5 copy.6
  336.1 194.4 %reduce-scatter.5.cloned.1.call-done = bf16[128,768]{1,0:T(8,128)(2,1)} async-done(((bf16[4096,768]{1,0:T(8,128)(2,1)}), bf16[128,768]{1,0:T(8,128)(2,1)}) %reduce-scatter.5.cloned.1.call-update) | async-done | bytes 196624 | tf_op jit(solution)/shard_map/reduce_scatter | solution.py:34
  530.6 0.9 copy.8
Async XLA Ops:
  7.2 72.9 %copy-start = (bf16[768,768]{1,0:T(8,128)(2,1)S(1)}, bf16[768,768]{1,0:T(8,128)(2,1)}, u32[]{:S(2)}) copy-start(bf16[768,768]{1,0:T(8,128)(2,1)} %param.4) | copy-start | bytes 3538948
  7.2 72.9 %all-gather.3.cloned.1.call-start = ((), (), s32[]{:S(2)}) async-start(), calls=%async_computation.2 | async-start | bytes 6488064 | tf_op jit(solution)/shard_map/all_gather | solution.py:24
  7.9 217.9 %reduce-scatter.3.cloned.1.call-start = ((), (), s32[]{:S(2)}) async-start(), calls=%async_computation.3 | async-start | bytes 7077888 | tf_op jit(solution)/shard_map/reduce_scatter | solution.py:27
  89.7 1.1 copy-start.1
  89.8 225.3 %all-gather.5.cloned.1.call-start = ((), (), s32[]{:S(2)}) async-start(), calls=%async_computation.4 | async-start | bytes 7077888 | tf_op jit(solution)/shard_map/all_gather | solution.py:33
  90.9 0.7 collective-permute-start.1
  228.7 301.8 %reduce-scatter.5.cloned.1.call-start = ((), (), s32[]{:S(2)}) async-start(), calls=%async_computation.5 | async-start | bytes 6488064 | tf_op jit(solution)/shard_map/reduce_scatter | solution.py:34
  324.9 0.7 collective-permute-start
Sparse Core Ops, SparseCore 0:
  9.9 70.1 all-gather.2
  89.9 135.8 reduce-scatter.2
  228.8 86.2 all-gather.4
  325.0 205.5 reduce-scatter.4

commit v2 on v1

v2 whole, which is shorter than its diff:
```python
import functools

import jax
import jax.numpy as jnp
from jax import lax
from jax.experimental import pallas as pl
from jax.experimental.pallas import tpu as pltpu
from jax.sharding import PartitionSpec as P

MESH = pl.DeviceIdType.MESH
inv_root_two = 0.7071067811865476
inv_root_tau = 0.3989422804014327

ORDER = (4, 3, 5, 2, 6, 1, 7, 0)
CHUNKS = 4


def plus(a, c):
    return lax.rem(lax.div(a, 4) + lax.div(c, 4), 2) * 4 + lax.rem(a + c, 4)


def minus(a, c):
    return lax.rem(lax.div(a, 4) - lax.div(c, 4) + 2, 2) * 4 + lax.rem(
        lax.rem(a, 4) - lax.rem(c, 4) + 4, 4
    )


def kernel(
    tok_ref, w_ref, cot_ref,
    act_ref, ig_ref, wg_ref,
    tokens, cot, given, taken, grads, act, total, near_out, near_in, far_out, far_in,
    t_send, t_recv, s_send, s_recv, c_send, c_recv, v_send, v_recv,
    r_send, r_recv, g_send, g_recv, n_send, n_recv, f_send, f_recv,
):
    a, q, b = lax.axis_index("gx"), lax.axis_index("gy"), lax.axis_index("gz")
    half, core = lax.div(q, 2), lax.rem(q, 2)
    piece = tok_ref.shape[0]
    rows = lambda r: pl.ds(pl.multiple_of(r * piece, piece), piece)
    at = lambda gx=a, gy=q, gz=b: {"gx": gx, "gy": gy, "gz": gz}
    up, down = lax.rem(b + 1, 8), lax.rem(b + 7, 8)
    sibling = at(gy=half * 2 + 1 - core)
    ahead = at(gx=a, gz=up), at(gx=a, gz=down)
    home = at(gx=plus(a, b), gz=a)
    source = at(gx=b, gz=minus(a, b))
    fixed = jnp.logical_and(a == 0, b == 0)
    moved = jnp.logical_not(fixed)
    offset = [lax.rem(b + o, 8) for o in ORDER]
    group = [plus(a, c) for c in offset]

    def remote(src, dst, send, recv, device):
        return pltpu.make_async_remote_copy(
            src_ref=src, dst_ref=dst, send_sem=send, recv_sem=recv, device_id=device, device_id_type=MESH
        )

    barrier = pltpu.get_barrier_semaphore()

    def greet(device):
        pl.semaphore_signal(barrier, inc=1, device_id=device, device_id_type=MESH)

    greet(at(gy=(1 - half) * 2 + core))
    greet(sibling)
    greet(ahead[0])
    greet(ahead[1])
    for c in range(1, 8):
        for j in range(2):
            greet(at(gx=plus(a, c), gy=j * 2 + core))

    @pl.when(moved)
    def _():
        greet(home)
        greet(source)

    pl.semaphore_wait(barrier, jnp.where(fixed, 18, 20))

    def token_copy(n, j):
        return remote(
            tok_ref, tokens.at[a, rows(q)], t_send.at[n * 2 + j], t_recv.at[n * 2 + half],
            at(gx=minus(a, offset[n]), gy=j * 2 + core),
        )

    def own(n, j):
        return jnp.logical_and(offset[n] == 0, half == j)

    def send_tokens(n):
        for j in range(2):

            @pl.when(jnp.logical_not(own(n, j)))
            def _():
                token_copy(n, j).start()

    def pass_copy(n, j, of):
        slot = tokens.at[group[n], rows(j * 2 + of)]
        return remote(slot, slot, s_send.at[n * 2 + j], s_recv.at[n * 2 + j], sibling)

    def get_tokens(n):
        for j in range(2):
            slot = tokens.at[group[n], rows(j * 2 + core)]

            @pl.when(jnp.logical_not(own(n, j)))
            def _():
                remote(slot, slot, t_send.at[n * 2 + j], t_recv.at[n * 2 + j], sibling).wait_recv()

            pass_copy(n, j, core).start()

    def get_passed(n):
        for j in range(2):
            pass_copy(n, j, 1 - core).wait_recv()

    def product(n, r):
        return jnp.dot(tokens[group[n], rows(r), :], w_ref[...], preferred_element_type=jnp.float32)

    def sum_copy(d, i):
        return remote(given.at[d, i], taken.at[d, i], r_send.at[d, i], r_recv.at[d, i], ahead[d])

    def place(d, p):
        return lax.rem(p + CHUNKS // 2, CHUNKS) if d == 0 else p

    def reduce_steps(first, last, base, n, add):
        def step(p, carry):
            i = base + p
            for d in range(2):
                value = product(n[d], place(d, p))
                if add:
                    sum_copy(d, i - CHUNKS).wait_recv()
                    value = value + taken[d, i - CHUNKS].astype(jnp.float32)
                given[d, i] = value.astype(jnp.bfloat16)
                sum_copy(d, i).start()
            return carry

        lax.fori_loop(first, last, step, 0)

    send_tokens(0)
    tokens[a, rows(q), :] = tok_ref[...]
    get_tokens(0)
    send_tokens(1)
    send_tokens(2)
    get_passed(0)

    cot_copy = remote(cot_ref, cot, c_send, c_recv, source)

    reduce_steps(2, 4, -2, (0, 0), False)

    @pl.when(moved)
    def _():
        cot_copy.start()

    @pl.when(fixed)
    def _():
        cot[...] = cot_ref[...]

    for k in (3, 2, 1):
        n = 7 - 2 * k
        get_tokens(n)
        get_tokens(n + 1)
        send_tokens(n + 2)
        if k > 1:
            send_tokens(n + 3)
        get_passed(n)
        get_passed(n + 1)
        base = (4 - k) * CHUNKS - 2
        if k == 3:
            reduce_steps(0, 2, base, (n, n + 1), False)
            reduce_steps(2, 4, base, (n, n + 1), True)
        else:
            reduce_steps(0, 4, base, (n, n + 1), True)
    get_tokens(7)
    get_passed(7)

    def own_product(r, carry):
        total[rows(r), :] = product(7, r)
        return carry

    lax.fori_loop(0, CHUNKS, own_product, 0)

    @pl.when(moved)
    def _():
        cot_copy.wait_recv()

    def grad_copy(d, u):
        k, p = lax.div(u, CHUNKS), lax.rem(u, CHUNKS)
        t = plus(a, lax.rem(b + 8 - k, 8) if d == 0 else lax.rem(b + k, 8))
        slot = grads.at[t, rows(p if d == 0 else lax.rem(p + CHUNKS // 2, CHUNKS))]
        return remote(slot, slot, g_send.at[d, u], g_recv.at[d, u], ahead[d])

    def grad_arrival(d, u):
        k, p = lax.div(u, CHUNKS) + 1, lax.rem(u, CHUNKS)
        t = plus(a, lax.rem(b + 8 - k, 8) if d == 0 else lax.rem(b + k, 8))
        slot = grads.at[t, rows(p if d == 0 else lax.rem(p + CHUNKS // 2, CHUNKS))]
        remote(slot, slot, g_send.at[d, u], g_recv.at[d, u], ahead[d]).wait_recv()

    def gelu_step(s, carry):
        r = lax.div(s, 2) + lax.rem(s, 2) * 2
        left = 10 + r
        right = 10 + lax.rem(r + 2, CHUNKS)
        sum_copy(0, right).wait_recv()
        sum_copy(1, left).wait_recv()
        x = total[rows(r), :] + taken[0, right].astype(jnp.float32) + taken[1, left].astype(jnp.float32)
        phi = 0.5 * (1.0 + lax.erf(x * inv_root_two))
        slope = phi + x * jnp.exp(-0.5 * x * x) * inv_root_tau
        act[rows(r), :] = (x * phi).astype(jnp.bfloat16)
        grads[group[7], rows(r), :] = (cot[rows(r), :].astype(jnp.float32) * slope).astype(jnp.bfloat16)
        grad_copy(0, r).start()
        grad_copy(1, lax.rem(r + 2, CHUNKS)).start()
        return carry

    lax.fori_loop(0, CHUNKS, gelu_step, 0)

    act_copy = remote(act, act_ref, v_send, v_recv, home)

    @pl.when(moved)
    def _():
        act_copy.start()

    @pl.when(fixed)
    def _():
        act_ref[...] = act[...]

    def near_copy(z, h):
        return remote(near_out.at[z * 2 + h], near_in.at[z * 2 + h], n_send.at[z * 2 + h], n_recv.at[z * 2 + h], sibling)

    def far_copy(z, h):
        return remote(
            far_out.at[z * 2 + h], far_in.at[z * 2 + half], f_send.at[z * 2 + h], f_recv.at[z * 2 + half],
            at(gx=plus(a, z), gy=h * 2 + core),
        )

    def far_own(z, h):
        return jnp.logical_and(z == 0, half == h)

    def back(t, r):
        return lax.dot_general(
            grads[t, rows(r), :], w_ref[...], (((1,), (1,)), ((), ())), preferred_element_type=jnp.float32
        )

    def give_near(z):
        def step(h, carry):
            near_out[z * 2 + h] = back(plus(a, z), h * 2 + 1 - core).astype(jnp.bfloat16)
            near_copy(z, h).start()
            return carry

        lax.fori_loop(0, 2, step, 0)

    def weigh(z, first=False):
        t = plus(a, z)

        def step(i, carry):
            columns = pl.ds(pl.multiple_of(i * 256, 256), 256)
            part = lax.dot_general(
                tokens[t, :, columns], grads[t], (((0,), (0,)), ((), ())), preferred_element_type=jnp.float32
            )
            total[columns, :] = part if first else total[columns, :] + part
            return carry

        lax.fori_loop(0, 3, step, 0)

    def give_far(z):
        def step(h, carry):
            value = back(plus(a, z), h * 2 + core)
            near_copy(z, h).wait_recv()
            value = (value + near_in[z * 2 + h].astype(jnp.float32)).astype(jnp.bfloat16)

            @pl.when(far_own(z, h))
            def _():
                far_in[z * 2 + half] = value

            @pl.when(jnp.logical_not(far_own(z, h)))
            def _():
                far_out[z * 2 + h] = value
                far_copy(z, h).start()

            return carry

        lax.fori_loop(0, 2, step, 0)

    give_near(b)
    weigh(b, True)
    give_far(b)
    for k in (1, 2, 3):

        def forward(p, carry):
            for d in range(2):
                grad_arrival(d, (k - 1) * CHUNKS + p)
                grad_copy(d, k * CHUNKS + p).start()
            return carry

        def keep(p, carry):
            for d in range(2):
                grad_arrival(d, (k - 1) * CHUNKS + p)
            return carry

        sent = CHUNKS if k < 3 else CHUNKS // 2
        lax.fori_loop(0, sent, forward, 0)
        lax.fori_loop(sent, CHUNKS, keep, 0)
        sides = lax.rem(b + 8 - k, 8), lax.rem(b + k, 8)
        for z in sides:
            give_near(z)
        for z in sides:
            weigh(z)
            give_far(z)

    def keep_last(p, carry):
        for d in range(2):
            grad_arrival(d, 3 * CHUNKS + p)
        return carry

    lax.fori_loop(0, CHUNKS // 2, keep_last, 0)
    opposite = lax.rem(b + 4, 8)
    give_near(opposite)
    give_far(opposite)
    weigh(opposite)

    def round_weight(i, carry):
        r = pl.ds(pl.multiple_of(i * 128, 128), 128)
        wg_ref[r, :] = total[r, :].astype(jnp.bfloat16)
        return carry

    lax.fori_loop(0, 6, round_weight, 0)

    def far_arrival(z, j):
        @pl.when(jnp.logical_not(far_own(z, j)))
        def _():
            slot = z * 2 + j
            remote(far_out.at[slot], far_in.at[slot], f_send.at[slot], f_recv.at[slot], sibling).wait_recv()

    def arrivals(z, carry):
        far_arrival(z, 0)
        far_arrival(z, 1)
        return carry

    lax.fori_loop(0, 8, arrivals, 0)

    def add_up(i, carry):
        r = pl.ds(pl.multiple_of(i * 16, 16), 16)
        value = far_in[0, r, :].astype(jnp.float32)
        for s in range(1, 16):
            value = value + far_in[s, r, :].astype(jnp.float32)
        ig_ref[r, :] = value.astype(jnp.bfloat16)
        return carry

    lax.fori_loop(0, piece // 16, add_up, 0)

    @pl.when(moved)
    def _():
        cot_copy.wait_send()
        act_copy.wait()

    for n in range(8):
        for j in range(2):
            pass_copy(n, j, core).wait_send()

            @pl.when(jnp.logical_not(own(n, j)))
            def _():
                token_copy(n, j).wait_send()

    def sent_sums(i, carry):
        for d in range(2):
            sum_copy(d, i).wait_send()
            grad_copy(d, i).wait_send()
        return carry

    lax.fori_loop(0, 14, sent_sums, 0)

    def sent_parts(z, carry):
        for h in range(2):
            near_copy(z, h).wait_send()

            @pl.when(jnp.logical_not(far_own(z, h)))
            def _():
                far_copy(z, h).wait_send()

        return carry

    lax.fori_loop(0, 8, sent_parts, 0)


def on_device(tokens, weight, cotangent):
    (piece, depth), (group, units) = tokens.shape, cotangent.shape
    bf16 = jnp.bfloat16
    shape = jax.ShapeDtypeStruct
    vmem = pl.BlockSpec(memory_space=pltpu.VMEM)
    dma = pltpu.SemaphoreType.DMA
    return pl.pallas_call(
        kernel,
        out_shape=(shape(cotangent.shape, bf16), shape(tokens.shape, bf16), shape(weight.shape, bf16)),
        in_specs=[vmem] * 3,
        out_specs=(vmem,) * 3,
        scratch_shapes=[
            pltpu.VMEM((8, group, depth), bf16),
            pltpu.VMEM((group, units), bf16),
            pltpu.VMEM((2, 14, piece, units), bf16),
            pltpu.VMEM((2, 14, piece, units), bf16),
            pltpu.VMEM((8, group, units), bf16),
            pltpu.VMEM((group, units), bf16),
            pltpu.VMEM((depth, units), jnp.float32),
            pltpu.VMEM((16, piece, depth), bf16),
            pltpu.VMEM((16, piece, depth), bf16),
            pltpu.VMEM((16, piece, depth), bf16),
            pltpu.VMEM((16, piece, depth), bf16),
            dma((16,)), dma((16,)), dma((16,)), dma((16,)),
            dma, dma, dma, dma,
            dma((2, 14)), dma((2, 14)), dma((2, 14)), dma((2, 14)),
            dma((16,)), dma((16,)), dma((16,)), dma((16,)),
        ],
        compiler_params=pltpu.CompilerParams(
            collective_id=0, has_side_effects=True, vmem_limit_bytes=60 * 1024 * 1024
        ),
    )(tokens, weight, cotangent)


def solution(mesh):
    in_specs = (P(("gx", "gy"), "gz"), P("gz", ("gy", "gx")), P("gx", ("gy", "gz")))
    out_specs = (P("gx", ("gy", "gz")), P(("gx", "gy"), "gz"), P("gz", ("gy", "gx")))
    return jax.shard_map(
        on_device, mesh=mesh, in_specs=in_specs, out_specs=out_specs, check_vma=False
    )
```

time: 541 us -> 287 us (0.53)
  the two profiles are of different devices: /device:TPU:1 before, /device:TPU:135 now
where the time goes in v2:
time: 287 us
  Pallas kernels  283 us (99%)
  local copies, waits for them, and re-layouts  3.87 us (1%)
    pallas_call x1, Pallas kernels, on_device(): pl.pallas_call(kernel, out_shape=(shape(cotangent.shape, bf16), shape(tok...  283 us

profile of v2, /device:TPU:135, one launch (start us, length us, event | category | flops | bytes accessed | tf_op | source)
XLA Modules:
  0.0 287.1 jit_solution(14193261073382358399)
XLA Ops:
  0.6 282.5 %shard_map.58 = (bf16[512,768]{1,0:T(8,128)(2,1)}, bf16[128,768]{1,0:T(8,128)(2,1)}, bf16[768,768]{1,0:T(8,128)(2,1)}) custom-call(bf16[128,768]{1,0:T(8,128)(2,1)} %tok_ref.1, bf16[768,768]{1,0:T(8,128)(2,1)} %w_ref.1, bf16[512,768]{1,0:T(8,128)(2,1)} %cot_ref.1), custom_call_target="tpu_custom_call" | custom-call | tf_op jit(solution)/shard_map/pallas_call | solution.py:382
  283.2 0.0 copy-start.1
  283.2 0.0 copy-start
  283.2 2.2 copy.9
  285.4 0.0 copy-done.1
  285.4 0.7 copy.10
  286.1 0.0 copy-done
  286.1 1.0 copy.11
Async XLA Ops:
  283.2 2.2 copy-start.1
  283.2 2.9 copy-start

commit v3 on v2

--- a/solution.py
+++ b/solution.py
@@ -11,25 +11,42 @@
 inv_root_two = 0.7071067811865476
 inv_root_tau = 0.3989422804014327
 
+LANDING = (
+    (1, 3, 5, 2, 0, 7, 4, 6),
+    (7, 2, 4, 3, 6, 1, 5, 0),
+    (6, 4, 2, 0, 7, 5, 1, 3),
+    (2, 7, 6, 1, 4, 3, 0, 5),
+    (0, 5, 3, 6, 1, 4, 7, 2),
+    (3, 1, 0, 7, 5, 2, 6, 4),
+    (5, 0, 1, 4, 3, 6, 2, 7),
+    (4, 6, 7, 5, 2, 0, 3, 1),
+)
+Z_OF = tuple(tuple(LANDING[a].index(t) for t in range(8)) for a in range(8))
+UNITS_OF = tuple(tuple([row[b] for row in LANDING].index(t) for b in range(8)) for t in range(8))
 ORDER = (4, 3, 5, 2, 6, 1, 7, 0)
 CHUNKS = 4
 
 
-def plus(a, c):
-    return lax.rem(lax.div(a, 4) + lax.div(c, 4), 2) * 4 + lax.rem(a + c, 4)
-
-
-def minus(a, c):
-    return lax.rem(lax.div(a, 4) - lax.div(c, 4) + 2, 2) * 4 + lax.rem(
-        lax.rem(a, 4) - lax.rem(c, 4) + 4, 4
-    )
+def choose(values, i):
+    value = values[0]
+    for k in range(1, len(values)):
+        value = jnp.where(i == k, values[k], value)
+    return value
+
+
+def row_of(table, i):
+    return choose([sum(v * 8**k for k, v in enumerate(row)) for row in table], i)
+
+
+def entry(row, k):
+    return lax.rem(lax.div(row, choose([8**p for p in range(8)], k)), 8)
 
 
 def kernel(
     tok_ref, w_ref, cot_ref,
     act_ref, ig_ref, wg_ref,
-    tokens, cot, given, taken, grads, act, total, near_out, near_in, far_out, far_in,
-    t_send, t_recv, s_send, s_recv, c_send, c_recv, v_send, v_recv,
+    tokens, cot, cot_mid, act_mid, given, taken, grads, act, total, near_out, near_in, far_out, far_in,
+    t_send, t_recv, s_send, s_recv, m_send, m_recv,
     r_send, r_recv, g_send, g_recv, n_send, n_recv, f_send, f_recv,
 ):
     a, q, b = lax.axis_index("gx"), lax.axis_index("gy"), lax.axis_index("gz")
@@ -40,12 +57,14 @@
     up, down = lax.rem(b + 1, 8), lax.rem(b + 7, 8)
     sibling = at(gy=half * 2 + 1 - core)
     ahead = at(gx=a, gz=up), at(gx=a, gz=down)
-    home = at(gx=plus(a, b), gz=a)
-    source = at(gx=b, gz=minus(a, b))
-    fixed = jnp.logical_and(a == 0, b == 0)
-    moved = jnp.logical_not(fixed)
+    landings = row_of(LANDING, a)
+    land = lambda z: entry(landings, z)
+    units = entry(row_of(UNITS_OF, a), b)
+    place_z = entry(row_of(Z_OF, b), a)
+    turned, shifted = place_z != b, units != a
+    x, y = half * 2 + lax.div(a, 4), lax.rem(a, 4)
     offset = [lax.rem(b + o, 8) for o in ORDER]
-    group = [plus(a, c) for c in offset]
+    group = [land(c) for c in offset]
 
     def remote(src, dst, send, recv, device):
         return pltpu.make_async_remote_copy(
@@ -63,48 +82,128 @@
     greet(ahead[1])
     for c in range(1, 8):
         for j in range(2):
-            greet(at(gx=plus(a, c), gy=j * 2 + core))
-
-    @pl.when(moved)
+            greet(at(gx=lax.rem(a + c, 8), gy=j * 2 + core))
+
+    @pl.when(turned)
     def _():
-        greet(home)
-        greet(source)
-
-    pl.semaphore_wait(barrier, jnp.where(fixed, 18, 20))
-
-    def token_copy(n, j):
-        return remote(
-            tok_ref, tokens.at[a, rows(q)], t_send.at[n * 2 + j], t_recv.at[n * 2 + half],
-            at(gx=minus(a, offset[n]), gy=j * 2 + core),
-        )
-
-    def own(n, j):
-        return jnp.logical_and(offset[n] == 0, half == j)
-
-    def send_tokens(n):
-        for j in range(2):
-
-            @pl.when(jnp.logical_not(own(n, j)))
-            def _():
-                token_copy(n, j).start()
-
-    def pass_copy(n, j, of):
-        slot = tokens.at[group[n], rows(j * 2 + of)]
-        return remote(slot, slot, s_send.at[n * 2 + j], s_recv.at[n * 2 + j], sibling)
-
-    def get_tokens(n):
-        for j in range(2):
-            slot = tokens.at[group[n], rows(j * 2 + core)]
-
-            @pl.when(jnp.logical_not(own(n, j)))
-            def _():
-                remote(slot, slot, t_send.at[n * 2 + j], t_recv.at[n * 2 + j], sibling).wait_recv()
-
-            pass_copy(n, j, core).start()
-
-    def get_passed(n):
-        for j in range(2):
-            pass_copy(n, j, 1 - core).wait_recv()
+        greet(at(gz=place_z))
+        greet(at(gz=units))
+
+    pl.semaphore_wait(barrier, jnp.where(turned, 20, 18))
+
+    side = piece // 2
+
+    def spot(i, j, s, lo=0, n=side, of=core):
+        px, py = lax.rem(x + i, 4), lax.rem(y + j, 4)
+        row = (lax.div(px, 2) * 2 + of) * piece + s * side + lo
+        return tokens.at[lax.rem(px, 2) * 4 + py, pl.ds(pl.multiple_of(row, side // 2), n)]
+
+    def chip(i, j):
+        px, py = lax.rem(x + i, 4), lax.rem(y + j, 4)
+        return at(gx=lax.rem(px, 2) * 4 + py, gy=lax.div(px, 2) * 2 + core)
+
+    def from_whom(w):
+        return 1 if w in (0, 3) else 3
+
+    def what(w):
+        return ((1, 0, side), (3, 0, side), (2, 0, side // 2), (2, side // 2, side // 2))[w]
+
+    def first_copy(s, w, arrival):
+        e, lo, n = what(w)
+        to = 4 - from_whom(w)
+        if not arrival:
+            e = (e + to) % 4
+        slot = spot(e, 0, s, lo, n) if s == 0 else spot(0, e, s, lo, n)
+        i = s * 4 + w
+        return remote(slot, slot, t_send.at[i], t_recv.at[i], chip(to, 0) if s == 0 else chip(0, to))
+
+    def second_copy(s, e, w, arrival):
+        f, lo, n = what(w)
+        to = 4 - from_whom(w)
+        if not arrival:
+            f = (f + to) % 4
+        slot = spot(e, f, s, lo, n) if s == 0 else spot(f, e, s, lo, n)
+        i = 8 + s * 16 + e * 4 + w
+        return remote(slot, slot, t_send.at[i], t_recv.at[i], chip(0, to) if s == 0 else chip(to, 0))
+
+    def pass_copy(s, e, f, of):
+        slot = spot(e, f, s, of=of) if s == 0 else spot(f, e, s, of=of)
+        i = s * 16 + e * 4 + f
+        return remote(slot, slot, s_send.at[i], s_recv.at[i], sibling)
+
+    def give_second(e):
+        for s in range(2):
+            second_copy(s, e, 0, False).start()
+            second_copy(s, e, 1, False).start()
+            pass_copy(s, e, 0, core).start()
+
+    def relay_second(e):
+        for s in range(2):
+            for w in range(2):
+                second_copy(s, e, w, True).wait_recv()
+                second_copy(s, e, 3 - w, False).start()
+                pass_copy(s, e, 1 + 2 * w, core).start()
+
+    def end_second(e):
+        for s in range(2):
+            second_copy(s, e, 2, True).wait_recv()
+            second_copy(s, e, 3, True).wait_recv()
+            pass_copy(s, e, 2, core).start()
+
+    def gather_tokens():
+        tokens[a, rows(q), :] = tok_ref[...]
+        for s in range(2):
+            first_copy(s, 0, False).start()
+            first_copy(s, 1, False).start()
+        give_second(0)
+        for w in range(2):
+            for s in range(2):
+                first_copy(s, w, True).wait_recv()
+                first_copy(s, 3 - w, False).start()
+            give_second(1 + 2 * w)
+        relay_second(0)
+        for s in range(2):
+            first_copy(s, 2, True).wait_recv()
+            first_copy(s, 3, True).wait_recv()
+        give_second(2)
+        for e in (1, 3):
+            relay_second(e)
+        end_second(0)
+        relay_second(2)
+        for e in (1, 3, 2):
+            end_second(e)
+        for s in range(2):
+            for e in range(4):
+                for f in range(4):
+                    pass_copy(s, e, f, 1 - core).wait_recv()
+
+    cot_turn = remote(cot_ref, cot_mid, m_send.at[0], m_recv.at[0], at(gz=place_z))
+    cot_shift = remote(cot_mid, cot, m_send.at[1], m_recv.at[1], at(gx=units))
+
+    def act_shift(r):
+        return remote(act.at[rows(r)], act_mid.at[rows(r)], m_send.at[2 + r], m_recv.at[2 + r], at(gx=land(b)))
+
+    def act_turn(r):
+        return remote(act_mid.at[rows(r)], act_ref.at[rows(r)], m_send.at[6 + r], m_recv.at[6 + r], at(gz=units))
+
+    def set_off(copy, leaves, src, dst, r=slice(None)):
+        @pl.when(leaves)
+        def _():
+            copy.start()
+
+        @pl.when(jnp.logical_not(leaves))
+        def _():
+            dst[r, :] = src[r, :]
+
+    def arrived(copy, leaves):
+        @pl.when(leaves)
+        def _():
+            copy.wait_recv()
+
+    def departed(copy, leaves):
+        @pl.when(leaves)
+        def _():
+            copy.wait_send()
 
     def product(n, r):
         return jnp.dot(tokens[group[n], rows(r), :], w_ref[...], preferred_element_type=jnp.float32)
@@ -129,42 +228,19 @@
 
         lax.fori_loop(first, last, step, 0)
 
-    send_tokens(0)
-    tokens[a, rows(q), :] = tok_ref[...]
-    get_tokens(0)
-    send_tokens(1)
-    send_tokens(2)
-    get_passed(0)
-
-    cot_copy = remote(cot_ref, cot, c_send, c_recv, source)
-
+    set_off(cot_turn, turned, cot_ref, cot_mid)
+    gather_tokens()
     reduce_steps(2, 4, -2, (0, 0), False)
-
-    @pl.when(moved)
-    def _():
-        cot_copy.start()
-
-    @pl.when(fixed)
-    def _():
-        cot[...] = cot_ref[...]
-
+    arrived(cot_turn, turned)
+    set_off(cot_shift, shifted, cot_mid, cot)
     for k in (3, 2, 1):
         n = 7 - 2 * k
-        get_tokens(n)
-        get_tokens(n + 1)
-        send_tokens(n + 2)
-        if k > 1:
-            send_tokens(n + 3)
-        get_passed(n)
-        get_passed(n + 1)
         base = (4 - k) * CHUNKS - 2
         if k == 3:
             reduce_steps(0, 2, base, (n, n + 1), False)
             reduce_steps(2, 4, base, (n, n + 1), True)
         else:
             reduce_steps(0, 4, base, (n, n + 1), True)
-    get_tokens(7)
-    get_passed(7)
 
     def own_product(r, carry):
         total[rows(r), :] = product(7, r)
@@ -172,19 +248,17 @@
 
     lax.fori_loop(0, CHUNKS, own_product, 0)
 
-    @pl.when(moved)
-    def _():
-        cot_copy.wait_recv()
+    arrived(cot_shift, shifted)
 
     def grad_copy(d, u):
         k, p = lax.div(u, CHUNKS), lax.rem(u, CHUNKS)
-        t = plus(a, lax.rem(b + 8 - k, 8) if d == 0 else lax.rem(b + k, 8))
+        t = land(lax.rem(b + 8 - k, 8) if d == 0 else lax.rem(b + k, 8))
         slot = grads.at[t, rows(p if d == 0 else lax.rem(p + CHUNKS // 2, CHUNKS))]
         return remote(slot, slot, g_send.at[d, u], g_recv.at[d, u], ahead[d])
 
     def grad_arrival(d, u):
         k, p = lax.div(u, CHUNKS) + 1, lax.rem(u, CHUNKS)
-        t = plus(a, lax.rem(b + 8 - k, 8) if d == 0 else lax.rem(b + k, 8))
+        t = land(lax.rem(b + 8 - k, 8) if d == 0 else lax.rem(b + k, 8))
         slot = grads.at[t, rows(p if d == 0 else lax.rem(p + CHUNKS // 2, CHUNKS))]
         remote(slot, slot, g_send.at[d, u], g_recv.at[d, u], ahead[d]).wait_recv()
 
@@ -201,19 +275,10 @@
         grads[group[7], rows(r), :] = (cot[rows(r), :].astype(jnp.float32) * slope).astype(jnp.bfloat16)
         grad_copy(0, r).start()
         grad_copy(1, lax.rem(r + 2, CHUNKS)).start()
+        set_off(act_shift(r), shifted, act, act_mid, rows(r))
         return carry
 
     lax.fori_loop(0, CHUNKS, gelu_step, 0)
-
-    act_copy = remote(act, act_ref, v_send, v_recv, home)
-
-    @pl.when(moved)
-    def _():
-        act_copy.start()
-
-    @pl.when(fixed)
-    def _():
-        act_ref[...] = act[...]
 
     def near_copy(z, h):
         return remote(near_out.at[z * 2 + h], near_in.at[z * 2 + h], n_send.at[z * 2 + h], n_recv.at[z * 2 + h], sibling)
@@ -221,11 +286,11 @@
     def far_copy(z, h):
         return remote(
             far_out.at[z * 2 + h], far_in.at[z * 2 + half], f_send.at[z * 2 + h], f_recv.at[z * 2 + half],
-            at(gx=plus(a, z), gy=h * 2 + core),
+            at(gx=land(z), gy=h * 2 + core),
         )
 
     def far_own(z, h):
-        return jnp.logical_and(z == 0, half == h)
+        return jnp.logical_and(land(z) == a, half == h)
 
     def back(t, r):
         return lax.dot_general(
@@ -234,14 +299,14 @@
 
     def give_near(z):
         def step(h, carry):
-            near_out[z * 2 + h] = back(plus(a, z), h * 2 + 1 - core).astype(jnp.bfloat16)
+            near_out[z * 2 + h] = back(land(z), h * 2 + 1 - core).astype(jnp.bfloat16)
             near_copy(z, h).start()
             return carry
 
         lax.fori_loop(0, 2, step, 0)
 
     def weigh(z, first=False):
-        t = plus(a, z)
+        t = land(z)
 
         def step(i, carry):
             columns = pl.ds(pl.multiple_of(i * 256, 256), 256)
@@ -255,7 +320,7 @@
 
     def give_far(z):
         def step(h, carry):
-            value = back(plus(a, z), h * 2 + core)
+            value = back(land(z), h * 2 + core)
             near_copy(z, h).wait_recv()
             value = (value + near_in[z * 2 + h].astype(jnp.float32)).astype(jnp.bfloat16)
 
@@ -281,6 +346,9 @@
             for d in range(2):
                 grad_arrival(d, (k - 1) * CHUNKS + p)
                 grad_copy(d, k * CHUNKS + p).start()
+            if k == 2:
+                arrived(act_shift(p), shifted)
+                set_off(act_turn(p), turned, act_mid, act_ref, rows(p))
             return carry
 
         def keep(p, carry):
@@ -339,18 +407,19 @@
 
     lax.fori_loop(0, piece // 16, add_up, 0)
 
-    @pl.when(moved)
-    def _():
-        cot_copy.wait_send()
-        act_copy.wait()
-
-    for n in range(8):
-        for j in range(2):
-            pass_copy(n, j, core).wait_send()
-
-            @pl.when(jnp.logical_not(own(n, j)))
-            def _():
-                token_copy(n, j).wait_send()
+    departed(cot_turn, turned)
+    departed(cot_shift, shifted)
+    for r in range(CHUNKS):
+        arrived(act_turn(r), turned)
+        departed(act_turn(r), turned)
+        departed(act_shift(r), shifted)
+    for s in range(2):
+        for w in range(4):
+            first_copy(s, w, False).wait_send()
+        for e in range(4):
+            for w in range(4):
+                second_copy(s, e, w, False).wait_send()
+                pass_copy(s, e, w, core).wait_send()
 
     def sent_sums(i, carry):
         for d in range(2):
@@ -387,6 +456,8 @@
         scratch_shapes=[
             pltpu.VMEM((8, group, depth), bf16),
             pltpu.VMEM((group, units), bf16),
+            pltpu.VMEM((group, units), bf16),
+            pltpu.VMEM((group, units), bf16),
             pltpu.VMEM((2, 14, piece, units), bf16),
             pltpu.VMEM((2, 14, piece, units), bf16),
             pltpu.VMEM((8, group, units), bf16),
@@ -396,8 +467,8 @@
             pltpu.VMEM((16, piece, depth), bf16),
             pltpu.VMEM((16, piece, depth), bf16),
             pltpu.VMEM((16, piece, depth), bf16),
-            dma((16,)), dma((16,)), dma((16,)), dma((16,)),
-            dma, dma, dma, dma,
+            dma((40,)), dma((40,)), dma((32,)), dma((32,)),
+            dma((10,)), dma((10,)),
             dma((2, 14)), dma((2, 14)), dma((2, 14)), dma((2, 14)),
             dma((16,)), dma((16,)), dma((16,)), dma((16,)),
         ],

time: 287 us -> 220 us (0.77)
  the two profiles are of different devices: /device:TPU:135 before, /device:TPU:1 now
where the time goes in v3:
time: 220 us; the launch traced here: 219 us
  Pallas kernels  214 us (97%)
  local copies, waits for them, and re-layouts  3.87 us (2%)
    pallas_call x1, Pallas kernels, on_device(): pl.pallas_call(kernel, out_shape=(shape(cotangent.shape, bf16), shape(tok...  214 us

profile of v3, /device:TPU:1, one launch (start us, length us, event | category | flops | bytes accessed | tf_op | source)
XLA Modules:
  0.0 219.0 jit_solution(7118454663986517035)
XLA Ops:
  0.6 214.4 %shard_map.58 = (bf16[512,768]{1,0:T(8,128)(2,1)}, bf16[128,768]{1,0:T(8,128)(2,1)}, bf16[768,768]{1,0:T(8,128)(2,1)}) custom-call(bf16[128,768]{1,0:T(8,128)(2,1)} %tok_ref.1, bf16[768,768]{1,0:T(8,128)(2,1)} %w_ref.1, bf16[512,768]{1,0:T(8,128)(2,1)} %cot_ref.1), custom_call_target="tpu_custom_call" | custom-call | tf_op jit(solution)/shard_map/pallas_call | solution.py:451
  215.1 0.0 copy-start.1
  215.1 0.0 copy-start
  215.1 2.2 copy.9
  217.3 0.0 copy-done.1
  217.3 0.7 copy.10
  218.0 0.0 copy-done
  218.0 1.0 copy.11
Async XLA Ops:
  215.1 2.2 %copy-start.1 = (bf16[128,768]{1,0:T(8,128)(2,1)S(1)}, bf16[128,768]{1,0:T(8,128)(2,1)}, u32[]{:S(2)}) copy-start(bf16[128,768]{1,0:T(8,128)(2,1)} %get-tuple-element.7) | copy-start | bytes 589828
  215.1 2.9 %copy-start = (bf16[768,768]{1,0:T(8,128)(2,1)S(1)}, bf16[768,768]{1,0:T(8,128)(2,1)}, u32[]{:S(2)}) copy-start(bf16[768,768]{1,0:T(8,128)(2,1)} %get-tuple-element.8) | copy-start | bytes 3538948

commit v4 on v3

--- a/solution.py
+++ b/solution.py
@@ -12,14 +12,14 @@
 inv_root_tau = 0.3989422804014327
 
 LANDING = (
-    (1, 3, 5, 2, 0, 7, 4, 6),
-    (7, 2, 4, 3, 6, 1, 5, 0),
-    (6, 4, 2, 0, 7, 5, 1, 3),
-    (2, 7, 6, 1, 4, 3, 0, 5),
-    (0, 5, 3, 6, 1, 4, 7, 2),
-    (3, 1, 0, 7, 5, 2, 6, 4),
-    (5, 0, 1, 4, 3, 6, 2, 7),
-    (4, 6, 7, 5, 2, 0, 3, 1),
+    (2, 5, 4, 3, 6, 1, 0, 7),
+    (1, 2, 7, 0, 5, 6, 3, 4),
+    (0, 3, 6, 1, 4, 7, 2, 5),
+    (7, 4, 5, 6, 3, 0, 1, 2),
+    (6, 1, 0, 7, 2, 5, 4, 3),
+    (5, 6, 3, 4, 1, 2, 7, 0),
+    (4, 7, 2, 5, 0, 3, 6, 1),
+    (3, 0, 1, 2, 7, 4, 5, 6),
 )
 Z_OF = tuple(tuple(LANDING[a].index(t) for t in range(8)) for a in range(8))
 UNITS_OF = tuple(tuple([row[b] for row in LANDING].index(t) for b in range(8)) for t in range(8))
@@ -150,18 +150,58 @@
             second_copy(s, e, 3, True).wait_recv()
             pass_copy(s, e, 2, core).start()
 
+    cot_shift = remote(cot_mid, cot, m_send.at[1], m_recv.at[1], at(gx=units))
+
+    def cot_turn(r):
+        return remote(cot_ref.at[rows(r)], cot_mid.at[rows(r)], m_send.at[10 + r], m_recv.at[10 + r], at(gz=place_z))
+
+    def act_shift(r):
+        return remote(act.at[rows(r)], act_mid.at[rows(r)], m_send.at[2 + r], m_recv.at[2 + r], at(gx=land(b)))
+
+    def act_turn(r):
+        return remote(act_mid.at[rows(r)], act_ref.at[rows(r)], m_send.at[6 + r], m_recv.at[6 + r], at(gz=units))
+
+    def set_off(copy, leaves, src, dst, r=slice(None)):
+        @pl.when(leaves)
+        def _():
+            copy.start()
+
+        @pl.when(jnp.logical_not(leaves))
+        def _():
+            dst[r, :] = src[r, :]
+
+    def arrived(copy, leaves):
+        @pl.when(leaves)
+        def _():
+            copy.wait_recv()
+
+    def departed(copy, leaves):
+        @pl.when(leaves)
+        def _():
+            copy.wait_send()
+
+    def turn_act(r):
+        arrived(act_shift(r), shifted)
+        set_off(act_turn(r), turned, act_mid, act_ref, rows(r))
+
+    def turn_cot(r):
+        set_off(cot_turn(r), turned, cot_ref, cot_mid, rows(r))
+
     def gather_tokens():
         tokens[a, rows(q), :] = tok_ref[...]
         for s in range(2):
             first_copy(s, 0, False).start()
             first_copy(s, 1, False).start()
         give_second(0)
+        turn_cot(0)
         for w in range(2):
             for s in range(2):
                 first_copy(s, w, True).wait_recv()
                 first_copy(s, 3 - w, False).start()
             give_second(1 + 2 * w)
+            turn_cot(1 + w)
         relay_second(0)
+        turn_cot(3)
         for s in range(2):
             first_copy(s, 2, True).wait_recv()
             first_copy(s, 3, True).wait_recv()
@@ -176,34 +216,6 @@
             for e in range(4):
                 for f in range(4):
                     pass_copy(s, e, f, 1 - core).wait_recv()
-
-    cot_turn = remote(cot_ref, cot_mid, m_send.at[0], m_recv.at[0], at(gz=place_z))
-    cot_shift = remote(cot_mid, cot, m_send.at[1], m_recv.at[1], at(gx=units))
-
-    def act_shift(r):
-        return remote(act.at[rows(r)], act_mid.at[rows(r)], m_send.at[2 + r], m_recv.at[2 + r], at(gx=land(b)))
-
-    def act_turn(r):
-        return remote(act_mid.at[rows(r)], act_ref.at[rows(r)], m_send.at[6 + r], m_recv.at[6 + r], at(gz=units))
-
-    def set_off(copy, leaves, src, dst, r=slice(None)):
-        @pl.when(leaves)
-        def _():
-            copy.start()
-
-        @pl.when(jnp.logical_not(leaves))
-        def _():
-            dst[r, :] = src[r, :]
-
-    def arrived(copy, leaves):
-        @pl.when(leaves)
-        def _():
-            copy.wait_recv()
-
-    def departed(copy, leaves):
-        @pl.when(leaves)
-        def _():
-            copy.wait_send()
 
     def product(n, r):
         return jnp.dot(tokens[group[n], rows(r), :], w_ref[...], preferred_element_type=jnp.float32)
@@ -228,12 +240,13 @@
 
         lax.fori_loop(first, last, step, 0)
 
-    set_off(cot_turn, turned, cot_ref, cot_mid)
     gather_tokens()
     reduce_steps(2, 4, -2, (0, 0), False)
-    arrived(cot_turn, turned)
-    set_off(cot_shift, shifted, cot_mid, cot)
     for k in (3, 2, 1):
+        if k == 2:
+            for r in range(CHUNKS):
+                arrived(cot_turn(r), turned)
+            set_off(cot_shift, shifted, cot_mid, cot)
         n = 7 - 2 * k
         base = (4 - k) * CHUNKS - 2
         if k == 3:
@@ -346,9 +359,8 @@
             for d in range(2):
                 grad_arrival(d, (k - 1) * CHUNKS + p)
                 grad_copy(d, k * CHUNKS + p).start()
-            if k == 2:
-                arrived(act_shift(p), shifted)
-                set_off(act_turn(p), turned, act_mid, act_ref, rows(p))
+            if k == 3:
+                turn_act(p)
             return carry
 
         def keep(p, carry):
@@ -369,6 +381,7 @@
     def keep_last(p, carry):
         for d in range(2):
             grad_arrival(d, 3 * CHUNKS + p)
+        turn_act(2 + p)
         return carry
 
     lax.fori_loop(0, CHUNKS // 2, keep_last, 0)
@@ -407,12 +420,12 @@
 
     lax.fori_loop(0, piece // 16, add_up, 0)
 
-    departed(cot_turn, turned)
     departed(cot_shift, shifted)
     for r in range(CHUNKS):
         arrived(act_turn(r), turned)
         departed(act_turn(r), turned)
         departed(act_shift(r), shifted)
+        departed(cot_turn(r), turned)
     for s in range(2):
         for w in range(4):
             first_copy(s, w, False).wait_send()
@@ -468,7 +481,7 @@
             pltpu.VMEM((16, piece, depth), bf16),
             pltpu.VMEM((16, piece, depth), bf16),
             dma((40,)), dma((40,)), dma((32,)), dma((32,)),
-            dma((10,)), dma((10,)),
+            dma((14,)), dma((14,)),
             dma((2, 14)), dma((2, 14)), dma((2, 14)), dma((2, 14)),
             dma((16,)), dma((16,)), dma((16,)), dma((16,)),
         ],

time: 220 us -> 187 us (0.85)
  the two profiles are of different devices: /device:TPU:1 before, /device:TPU:168 now
where the time goes in v4:
time: 187 us
  Pallas kernels  182 us (97%)
  local copies, waits for them, and re-layouts  3.87 us (2%)
    pallas_call x1, Pallas kernels, on_device(): pl.pallas_call(kernel, out_shape=(shape(cotangent.shape, bf16), shape(tok...  182 us
    unnamed x7, local copies, waits for them, and re-layouts  3.87 us

profile of v4, /device:TPU:168, one launch (start us, length us, event | category | flops | bytes accessed | tf_op | source)
XLA Modules:
  0.0 186.7 jit_solution(7772357163162786239)
XLA Ops:
  0.6 182.2 %shard_map.58 = (bf16[512,768]{1,0:T(8,128)(2,1)}, bf16[128,768]{1,0:T(8,128)(2,1)}, bf16[768,768]{1,0:T(8,128)(2,1)}) custom-call(bf16[128,768]{1,0:T(8,128)(2,1)} %tok_ref.1, bf16[768,768]{1,0:T(8,128)(2,1)} %w_ref.1, bf16[512,768]{1,0:T(8,128)(2,1)} %cot_ref.1), custom_call_target="tpu_custom_call" | custom-call | tf_op jit(solution)/shard_map/pallas_call | solution.py:464
  182.8 0.0 copy-start.1
  182.8 0.0 copy-start
  182.8 2.2 %copy.9 = bf16[512,768]{1,0:T(8,128)(2,1)} copy(bf16[512,768]{1,0:T(8,128)(2,1)} %get-tuple-element.6) | data formatting | bytes 1572864
  185.0 0.0 copy-done.1
  185.0 0.7 copy.10
  185.7 0.0 copy-done
  185.7 1.0 copy.11
Async XLA Ops:
  182.8 2.2 %copy-start.1 = (bf16[128,768]{1,0:T(8,128)(2,1)S(1)}, bf16[128,768]{1,0:T(8,128)(2,1)}, u32[]{:S(2)}) copy-start(bf16[128,768]{1,0:T(8,128)(2,1)} %get-tuple-element.7) | copy-start | bytes 589828
  182.8 2.9 %copy-start = (bf16[768,768]{1,0:T(8,128)(2,1)S(1)}, bf16[768,768]{1,0:T(8,128)(2,1)}, u32[]{:S(2)}) copy-start(bf16[768,768]{1,0:T(8,128)(2,1)} %get-tuple-element.8) | copy-start | bytes 3538948

commit v5 on v4

--- a/solution.py
+++ b/solution.py
@@ -193,15 +193,14 @@
             first_copy(s, 0, False).start()
             first_copy(s, 1, False).start()
         give_second(0)
-        turn_cot(0)
+        for r in range(CHUNKS):
+            turn_cot(r)
         for w in range(2):
             for s in range(2):
                 first_copy(s, w, True).wait_recv()
                 first_copy(s, 3 - w, False).start()
             give_second(1 + 2 * w)
-            turn_cot(1 + w)
         relay_second(0)
-        turn_cot(3)
         for s in range(2):
             first_copy(s, 2, True).wait_recv()
             first_copy(s, 3, True).wait_recv()
@@ -378,16 +377,20 @@
             weigh(z)
             give_far(z)
 
-    def keep_last(p, carry):
+    opposite = lax.rem(b + 4, 8)
+    for p in range(2):
         for d in range(2):
             grad_arrival(d, 3 * CHUNKS + p)
         turn_act(2 + p)
-        return carry
-
-    lax.fori_loop(0, CHUNKS // 2, keep_last, 0)
-    opposite = lax.rem(b + 4, 8)
-    give_near(opposite)
-    give_far(opposite)
+
+        @pl.when(core != p)
+        def _():
+            give_near(opposite)
+
+        @pl.when(core == p)
+        def _():
+            give_far(opposite)
+
     weigh(opposite)
 
     def round_weight(i, carry):

time: 187 us -> 184 us (0.984)
  the two profiles are of different devices: /device:TPU:168 before, /device:TPU:1 now
where the time goes in v5:
time: 184 us; the launch traced here: 181 us
  Pallas kernels  176 us (96%)
  local copies, waits for them, and re-layouts  3.87 us (2%)
    pallas_call x1, Pallas kernels, on_device(): pl.pallas_call(kernel, out_shape=(shape(cotangent.shape, bf16), shape(tok...  176 us
    unnamed x7, local copies, waits for them, and re-layouts  3.87 us

profile of v5, /device:TPU:1, one launch (start us, length us, event | category | flops | bytes accessed | tf_op | source)
XLA Modules:
  0.0 180.8 jit_solution(16274801850572860165)
XLA Ops:
  0.6 176.3 %shard_map.58 = (bf16[512,768]{1,0:T(8,128)(2,1)}, bf16[128,768]{1,0:T(8,128)(2,1)}, bf16[768,768]{1,0:T(8,128)(2,1)}) custom-call(bf16[128,768]{1,0:T(8,128)(2,1)} %tok_ref.1, bf16[768,768]{1,0:T(8,128)(2,1)} %w_ref.1, bf16[512,768]{1,0:T(8,128)(2,1)} %cot_ref.1), custom_call_target="tpu_custom_call" | custom-call | tf_op jit(solution)/shard_map/pallas_call | solution.py:467
  176.9 0.0 copy-start.1
  177.0 0.0 copy-start
  177.0 2.2 %copy.9 = bf16[512,768]{1,0:T(8,128)(2,1)} copy(bf16[512,768]{1,0:T(8,128)(2,1)} %get-tuple-element.6) | data formatting | bytes 1572864
  179.1 0.0 copy-done.1
  179.1 0.7 copy.10
  179.8 0.0 copy-done
  179.8 1.0 copy.11
Async XLA Ops:
  176.9 2.2 %copy-start.1 = (bf16[128,768]{1,0:T(8,128)(2,1)S(1)}, bf16[128,768]{1,0:T(8,128)(2,1)}, u32[]{:S(2)}) copy-start(bf16[128,768]{1,0:T(8,128)(2,1)} %get-tuple-element.7) | copy-start | bytes 589828
  177.0 2.9 %copy-start = (bf16[768,768]{1,0:T(8,128)(2,1)S(1)}, bf16[768,768]{1,0:T(8,128)(2,1)}, u32[]{:S(2)}) copy-start(bf16[768,768]{1,0:T(8,128)(2,1)} %get-tuple-element.8) | copy-start | bytes 3538948
